TPU v7x, 256 devices: a whole 4x4x8 slice. The times are simulated.
256 devices in a mesh: ia: 8 (over z), ja: 4 (over y), ka: 8 (over x, core).
Axes of the slice: x: 4, y: 4, z: 8, core: 2. Of those that a mesh axis runs over, the one named last changes fastest.
Arguments:
- blocks: bfloat16 [8, 4, 16, 128, 128, 128], P('ia', 'ja', 'ka'), may hold values from -6 to 6
- coordinates: int32 [3, 8, 4, 16], P(None, 'ia', 'ja', 'ka'), may hold values from 0 to 3, as said below
- occupancy: int32 [8, 4, 16], P('ia', 'ja', 'ka'), may hold values from 0 to 1, as said below
- second_factor: bfloat16 [4, 512, 1024], P('ja', ('ia', 'ka')), may hold values from -12 to 12
- third_factor: bfloat16 [8, 512, 1024], P('ka', ('ia', 'ja')), may hold values from -0.0234375 to 0.0234375
- inverse_first: bfloat16 [1024, 1024], replicated
- inverse_second: bfloat16 [1024, 1024], replicated
Outputs:
- first_new: bfloat16 [8, 512, 1024], P('ia', ('ja', 'ka'))
- second_new: bfloat16 [4, 512, 1024], P('ja', ('ia', 'ka'))
Inputs may be any that keep to these rules, and one draw needn't show every extreme that they name: `occupancy`: each device has two slots; its second slot is occupied only where its first is. A device with two blocks is followed along ka, cyclically, by a device with none. Some device holds two blocks. coordinates[0], [1], [2] of a slot are a block row among 4, a block row among 4 and a block layer among 4 of its device's ranges; the two slots of a device name different layers.
All inputs are finite; a program needn't handle non-finite values.
Results may differ from a plain program's by a relative error of at most 0.006.
Values may be sent and summed in bfloat16 or wider, within the bound.
No kernel may reach another device: no remote copies, remote signals or barrier semaphores. Data moves between devices by JAX's collectives and lax.ppermute only.
A program may use at most 128 MiB of HBM per device.

v0:
```python
import jax
import jax.numpy as jnp
from jax import lax
from jax.experimental import pallas as pl
from jax.experimental.pallas import tpu as pltpu
from jax.sharding import PartitionSpec as P

BLK = 128
CHUNK = 32
BF = jnp.bfloat16
F32 = jnp.float32


def rotated(x, axis, distance):
    n = lax.axis_size(axis)
    return lax.ppermute(x, axis, [(i, (i + distance) % n) for i in range(n)])


def core_swap(x):
    return lax.ppermute(x, "ka", [(i, i ^ 1) for i in range(lax.axis_size("ka"))])


def products(planes, group, rows, slab, acc, step):
    @pl.when(step == 0)
    def _():
        acc[...] = jnp.zeros_like(acc)

    left = rows[pl.ds(pl.multiple_of(step * CHUNK, CHUNK), CHUNK), :].astype(BF)
    width = acc.shape[-1] // 4
    for first in range(0, CHUNK, group):
        tiles = planes(first)
        lhs = jnp.concatenate([tiles[j] for j in range(group)], axis=1)
        for n in range(4):
            cols = slice(n * width, (n + 1) * width)
            layer = slab[:, cols]
            khatri = jnp.concatenate(
                [layer * left[j : j + 1, cols] for j in range(first, first + group)], axis=0
            )
            acc[:, cols] += jnp.dot(lhs, khatri, preferred_element_type=F32)


def for_slot(slot, when, todo):
    for s in range(2):

        @pl.when((slot == s) & when)
        def _():
            todo(s)


def layers_kernel(l0, l1, l2, l3, out_ref):
    for ref, distance in zip((l0, l1, l2, l3), (0, 1, 3, 2)):
        owner = lax.rem(lax.axis_index("ja") - distance + 4, 4)
        for s in range(2):
            for g in range(2):
                first = pl.multiple_of((g * 4 + owner) * 16, 16)
                out_ref[s, pl.ds(first, 16), :] = ref[s * 2 + g]


def layer_slabs(pieces):
    out = jax.ShapeDtypeStruct((2, BLK, pieces[0].shape[-1]), BF)
    return pl.pallas_call(
        layers_kernel,
        grid=(1,),
        in_specs=[pl.BlockSpec(memory_space=pltpu.VMEM)] * 4,
        out_specs=whole(out),
        out_shape=out,
        compiler_params=PARAMS,
        cost_estimate=pl.CostEstimate(
            flops=2 * 128**3 * 4096, bytes_accessed=2**20, transcendentals=0
        ),
    )(*pieces)


def first_kernel(
    sc, x_ref, own_ref, other_ref, tags_ref, slab_ref, out_ref, table_ref, rows, acc
):
    slot, step = pl.program_id(0), pl.program_id(1)

    @pl.when(step == 0)
    def _():
        col, c = sc[2 + slot], lax.axis_index("ka")
        for e, turn in enumerate((0, 2, 6, 4)):
            mine = lax.rem(c - turn + 8, 8)
            theirs = mine + 1 - 2 * lax.rem(c, 2)
            for h in range(2):
                for ref, owner in ((own_ref, mine), (other_ref, theirs)):
                    first = pl.multiple_of((h * 8 + owner) * 8, 8)
                    rows[pl.ds(first, 8), :] = ref[e, 2 * col + h].astype(F32)

    @pl.when((slot == 0) & (step == 0))
    def _():
        table_ref[...] = jnp.zeros_like(table_ref)
        for b in range(4):
            table_ref[pl.ds(b * 8 + lax.axis_index("ka"), 1), :] = tags_ref[b : b + 1, :]

    def planes(first):
        return jnp.swapaxes(x_ref[0, :, first : first + 16, :], 0, 1)

    products(planes, 16, rows, slab_ref.at[0], acc, step)

    def write(s):
        for b in range(4):
            for c in range(8):
                first = c * 16 + b * 4
                out_ref[b * 8 + c, s * 4 : s * 4 + 4] = acc[first : first + 4].astype(BF)

    for_slot(slot, step == pl.num_programs(1) - 1, write)


def second_kernel(
    x_hbm, inverse_hbm, got_ref, slabs_ref, out_ref, rows, acc, done, *fetched
):
    x_ref, inverse_ref, x_sems, inverse_sem = fetched

    def fetch(slot, step):
        part = pl.ds(pl.multiple_of(step * CHUNK, CHUNK), CHUNK)
        return pltpu.make_async_copy(
            x_hbm.at[slot, part], x_ref.at[slot, part], x_sems.at[slot, step]
        )

    for slot in range(2):
        for step in range(BLK // CHUNK):
            fetch(slot, step).start()
    inverse_copy = pltpu.make_async_copy(inverse_hbm, inverse_ref, inverse_sem)
    inverse_copy.start()
    for slot in range(2):
        for c in range(8):
            for b in range(4):
                first = c * 16 + b * 4
                rows[first : first + 4] = got_ref[b * 8 + c, slot * 4 : slot * 4 + 4].astype(F32)

        @pl.loop(0, BLK // CHUNK)
        def _(step):
            fetch(slot, step).wait()
            base = pl.multiple_of(step * CHUNK, CHUNK)
            products(
                lambda first: x_ref[slot, pl.ds(base + first, 32)],
                32,
                rows,
                slabs_ref.at[slot],
                acc,
                step,
            )

        done[slot * BLK : (slot + 1) * BLK] = acc[...].astype(BF)
    inverse_copy.wait()
    turned = jnp.dot(done[...], inverse_ref[...], preferred_element_type=F32).astype(BF)
    for slot in range(2):
        for c in range(8):
            for h in range(2):
                first, to = slot * BLK + h * 64 + c * 8, slot * 16 + h * 8
                out_ref[c, to : to + 8] = turned[first : first + 8]


PARAMS = pltpu.CompilerParams(vmem_limit_bytes=51 * 2**20)
COST = pl.CostEstimate(flops=2 * 2 * 128**3 * 1024, bytes_accessed=12 * 2**20, transcendentals=0)


def whole(x):
    return pl.BlockSpec(x.shape, lambda *ids: (0,) * len(x.shape))


def scratch_for(r):
    return [pltpu.VMEM((BLK, r), F32), pltpu.VMEM((BLK, r), F32)]


def first_products(scalars, x, others, slabs):
    r = others[0].shape[-1]
    outs = [jax.ShapeDtypeStruct((32, 8, r), BF), jax.ShapeDtypeStruct((32, 128), F32)]
    return pl.pallas_call(
        first_kernel,
        grid_spec=pltpu.PrefetchScalarGridSpec(
            num_scalar_prefetch=1,
            grid=(2, BLK // CHUNK),
            in_specs=[
                pl.BlockSpec((1, BLK, CHUNK, BLK), lambda s, q, sc: (s, 0, q, 0)),
                *[whole(o) for o in others],
                pl.BlockSpec((1, BLK, r), lambda s, q, sc: (s, 0, 0)),
            ],
            out_specs=[whole(o) for o in outs],
            scratch_shapes=scratch_for(r),
        ),
        out_shape=outs,
        compiler_params=PARAMS,
        cost_estimate=COST,
    )(scalars, x, *others, slabs)


def second_products(x, inverse, others):
    r = inverse.shape[0]
    out = jax.ShapeDtypeStruct((8, 32, r), BF)
    return pl.pallas_call(
        second_kernel,
        grid=(1,),
        in_specs=[
            *[pl.BlockSpec(memory_space=pltpu.HBM)] * 2,
            *[whole(o) for o in others],
        ],
        out_specs=whole(out),
        scratch_shapes=[
            *scratch_for(r),
            pltpu.VMEM((2 * BLK, r), BF),
            pltpu.VMEM(x.shape, BF),
            pltpu.VMEM((r, r), BF),
            pltpu.SemaphoreType.DMA((2, BLK // CHUNK)),
            pltpu.SemaphoreType.DMA(()),
        ],
        out_shape=out,
        compiler_params=PARAMS,
        cost_estimate=COST,
    )(x, inverse, *others)


def choose_kernel(sc, along_ref, *refs):
    *send_refs, rows_ref = refs
    for ref, distance in zip(send_refs, (0, 1, 3, 2)):
        to = lax.rem(lax.axis_index("ja") + distance, 4)
        for s in range(2):
            for g in range(2):
                ref[s * 2 + g] = along_ref[2 * sc[to * 2 + s] + g, 0:16]
    for a in range(8):
        rows_ref[a] = along_ref[a, 16:24]


def chosen_pieces(layers, along):
    r = along.shape[-1]
    outs = [jax.ShapeDtypeStruct((4, 16, r), BF)] * 4 + [jax.ShapeDtypeStruct((8, 8, r), BF)]
    return pl.pallas_call(
        choose_kernel,
        grid_spec=pltpu.PrefetchScalarGridSpec(
            num_scalar_prefetch=1,
            grid=(1,),
            in_specs=[whole(along)],
            out_specs=[whole(o) for o in outs],
        ),
        out_shape=outs,
        compiler_params=pltpu.CompilerParams(vmem_limit_bytes=16 * 2**20),
    )(layers, along)


def body(
    blocks, coordinates, occupancy, second_factor, third_factor, inverse_first, inverse_second
):
    r = inverse_first.shape[0]
    b, c = lax.axis_index("ja"), lax.axis_index("ka")
    own_blocks = blocks.reshape(2, BLK, BLK, BLK)
    places = coordinates.reshape(3, 2)

    mine = jnp.concatenate([third_factor[0], second_factor[0]], axis=0)
    along = lax.all_to_all(
        jnp.broadcast_to(mine, (8, *mine.shape)), "ia", 0, 0, tiled=True
    )
    tags = jnp.concatenate(
        [places.reshape(6), occupancy.reshape(2), jnp.zeros((120,), jnp.int32)]
    ).astype(F32)
    column = jnp.where((jnp.arange(4) == b)[:, None], tags[None, :], 0.0)
    column = column + rotated(column, "ja", 1) + rotated(column, "ja", 2) + rotated(column, "ja", 3)
    along, column = lax.optimization_barrier((along, column))

    layers = column[:, 4:6].reshape(8).astype(jnp.int32)
    *send, row_piece = chosen_pieces(layers, along)
    slabs = [send[0]] + [rotated(send[e], "ja", d) for e, d in ((1, 1), (2, 3), (3, 2))]
    own = [row_piece] + [rotated(row_piece, "ka", d) for d in (2, 6, 4)]
    slabs = layer_slabs(slabs)
    own = jnp.stack(own)
    other = core_swap(own)

    contribution, table = first_products(
        places.reshape(6), own_blocks, (own, other, column), slabs
    )

    arrived = lax.all_to_all(contribution, ("ja", "ka"), 0, 0, tiled=True)
    table = table + core_swap(table)
    table = table + rotated(table, "ka", 2) + rotated(table, "ka", 4) + rotated(table, "ka", 6)
    tag = jnp.repeat(table[:, 0:2].reshape(64), 4)
    weight = jnp.repeat(table[:, 6:8].reshape(64), 4)
    fine = jnp.arange(256) % 4
    owned_block, owned_fine = jnp.arange(16) // 4, jnp.arange(16) % 4
    match = (owned_block[:, None] == tag[None, :]) & (owned_fine[:, None] == fine[None, :])
    pick = jnp.where(match & (weight[None, :] > 0), 1, 0).astype(BF)
    give = jnp.where(match.T, 1, 0).astype(BF)
    owned = jnp.dot(pick, arrived.reshape(256, r), preferred_element_type=F32)
    new_rows = jnp.dot(owned.astype(BF), inverse_first, preferred_element_type=F32).astype(BF)
    sent = jnp.dot(give, new_rows, preferred_element_type=F32).astype(BF).reshape(32, 8, r)
    got = lax.all_to_all(sent, ("ja", "ka"), 0, 0, tiled=True)

    by_block = new_rows.reshape(4, 4, r)
    first_new = jnp.zeros((4, 4, r), BF)
    for d in range(4):
        piece = lax.dynamic_index_in_dim(by_block, (b + d) % 4, 0)
        if d:
            piece = rotated(piece, "ja", d)
        first_new = lax.dynamic_update_slice_in_dim(first_new, piece, (b - d) % 4, 0)
    first_new = first_new.reshape(1, 16, r)

    contribution = second_products(own_blocks, inverse_second, (got, slabs))
    arrived = lax.all_to_all(contribution, "ka", 0, 0, tiled=True)
    mine = lax.dynamic_slice_in_dim(table, b * 8, 8, 0)
    tag = jnp.repeat(mine[:, 2:4].reshape(16), 16)
    weight = jnp.repeat(mine[:, 6:8].reshape(16), 16)
    fine = jnp.arange(256) % 16
    owned_block, owned_fine = jnp.arange(64) // 16, jnp.arange(64) % 16
    match = (owned_block[:, None] == tag[None, :]) & (owned_fine[:, None] == fine[None, :])
    pick = jnp.where(match & (weight[None, :] > 0), 1, 0).astype(BF)
    partial = jnp.dot(pick, arrived.reshape(256, r), preferred_element_type=F32).astype(BF)
    last = lax.all_to_all(partial.reshape(8, 8, r), "ia", 0, 0, tiled=True)
    total = last[0].astype(F32)
    for a in range(1, 8):
        total = total + last[a].astype(F32)
    return first_new, total.astype(BF)[None]


def solution(mesh):
    in_specs = (
        P("ia", "ja", "ka", None, None, None),
        P(None, "ia", "ja", "ka"),
        P("ia", "ja", "ka"),
        P("ja", ("ia", "ka"), None),
        P("ka", ("ia", "ja"), None),
        P(),
        P(),
    )
    out_specs = (P("ia", ("ja", "ka"), None), P("ja", ("ia", "ka"), None))
    return jax.shard_map(body, mesh=mesh, in_specs=in_specs, out_specs=out_specs, check_vma=False)
```

profile of v0, /device:TPU:1, one launch (start us, length us, event | category | flops | bytes accessed | tf_op | source)
XLA Modules:
  0.0 132.5 jit_solution(9849648454889171452)
XLA Ops:
  0.6 0.9 pad_maximum_fusion.1
  1.6 0.8 broadcast_in_dim.75
  2.4 9.0 %all-to-all-start = ((bf16[8,24,1024]{2,1,0:T(8,128)(2,1)}), bf16[8,24,1024]{2,1,0:T(8,128)(2,1)S(1)}, u32[]{:S(2)}, u32[]{:S(2)}) async-start(bf16[8,24,1024]{2,1,0:T(8,128)(2,1)} %broadcast_in_dim.75), calls=%async_computation | async-start | bytes 786432 | tf_op jit(solution)/shard_map/all_to_all | solution.py:250
  11.4 0.8 copy.10
  12.2 0.1 reshape_reshape.4.sc
  12.2 0.7 add_convert_fusion.1
  13.0 0.1 broadcast_select_fusion
  13.1 1.3 collective-permute-start
  14.4 2.6 %collective-permute-start.1 = (f32[4,128]{1,0:T(4,128)S(1)}, f32[4,128]{1,0:T(4,128)S(1)}, u32[]{:S(2)}, u32[]{:S(2)}) collective-permute-start(f32[4,128]{1,0:T(4,128)S(1)} %broadcast_select_fusion), channel_id=1, source_target_pairs={{0,16},{8,24},{16,0},{24,8},{1,17},{9,25},{17,1},{25,9},{2,18},{10... | collective-permute-start | bytes 6152 | tf_op jit(solution)/shard_map/ppermute | solution.py:16
  17.0 1.1 collective-permute-start.2
  18.0 0.2 collective-permute-done.1
  18.3 1.4 %collective-permute-done.2 = f32[4,128]{1,0:T(4,128)S(1)} collective-permute-done((f32[4,128]{1,0:T(4,128)S(1)}, f32[4,128]{1,0:T(4,128)S(1)}, u32[]{:S(2)}, u32[]{:S(2)}) %collective-permute-start.2) | collective-permute-done | bytes 2080 | tf_op jit(solution)/shard_map/ppermute | solution.py:16
  19.7 0.1 add_add_fusion.1.tags_ref
  19.8 5.8 %all-to-all-done.along_ref = bf16[8,24,1024]{2,1,0:T(8,128)(2,1)S(1)} async-done(((bf16[8,24,1024]{2,1,0:T(8,128)(2,1)}), bf16[8,24,1024]{2,1,0:T(8,128)(2,1)S(1)}, u32[]{:S(2)}, u32[]{:S(2)}) %all-to-all-start) | async-done | bytes 393248 | tf_op jit(solution)/shard_map/all_to_all | solution.py:250
  25.6 0.1 slice_convert_fusion
  25.7 0.1 convert_element_type.90.sc
  25.7 0.6 shard_map.86
  26.3 1.3 collective-permute-start.3
  27.6 1.5 %collective-permute-start.4 = (bf16[8,8,1024]{2,1,0:T(8,128)(2,1)S(1)}, bf16[8,8,1024]{2,1,0:T(8,128)(2,1)S(1)}, u32[]{:S(2)}, u32[]{:S(2)}) collective-permute-start(bf16[8,8,1024]{2,1,0:T(8,128)(2,1)S(1)} %get-tuple-element.13), channel_id=1, source_target_pairs={{0,6},{1,7},{2,0},{3,1},{4,2},{5,3},{6,4},{7,5},{8,14},{9,15},{10,... | collective-permute-start | bytes 393224 | tf_op jit(solution)/shard_map/ppermute | solution.py:16
  29.1 1.5 %collective-permute-start.5 = (bf16[8,8,1024]{2,1,0:T(8,128)(2,1)S(1)}, bf16[8,8,1024]{2,1,0:T(8,128)(2,1)S(1)}, u32[]{:S(2)}, u32[]{:S(2)}) collective-permute-start(bf16[8,8,1024]{2,1,0:T(8,128)(2,1)S(1)} %get-tuple-element.13), channel_id=1, source_target_pairs={{0,4},{1,5},{2,6},{3,7},{4,0},{5,1},{6,2},{7,3},{8,12},{9,13},{10,... | collective-permute-start | bytes 393224 | tf_op jit(solution)/shard_map/ppermute | solution.py:16
  30.6 1.3 collective-permute-start.7
  31.9 1.4 %collective-permute-start.8 = (bf16[4,16,1024]{2,1,0:T(8,128)(2,1)S(1)}, bf16[4,16,1024]{2,1,0:T(8,128)(2,1)S(1)}, u32[]{:S(2)}, u32[]{:S(2)}) collective-permute-start(bf16[4,16,1024]{2,1,0:T(8,128)(2,1)S(1)} %get-tuple-element.16), channel_id=1, source_target_pairs={{0,24},{8,0},{16,8},{24,16},{1,25},{9,1},{17,9},{25,17},{2,26},{10... | collective-permute-start | bytes 393224 | tf_op jit(solution)/shard_map/ppermute | solution.py:16
  33.4 1.6 %collective-permute-start.9 = (bf16[4,16,1024]{2,1,0:T(8,128)(2,1)S(1)}, bf16[4,16,1024]{2,1,0:T(8,128)(2,1)S(1)}, u32[]{:S(2)}, u32[]{:S(2)}) collective-permute-start(bf16[4,16,1024]{2,1,0:T(8,128)(2,1)S(1)} %get-tuple-element.17), channel_id=1, source_target_pairs={{0,16},{8,24},{16,0},{24,8},{1,17},{9,25},{17,1},{25,9},{2,18},{10... | collective-permute-start | bytes 393224 | tf_op jit(solution)/shard_map/ppermute | solution.py:16
  35.0 1.1 collective-permute-done.5
  36.2 2.1 %collective-permute-start.6 = (bf16[4,8,8,1024]{3,2,1,0:T(8,128)(2,1)S(1)}, bf16[4,8,8,1024]{3,2,1,0:T(8,128)(2,1)S(1)}, u32[]{:S(2)}, u32[]{:S(2)}) collective-permute-start(bf16[4,8,8,1024]{3,2,1,0:T(8,128)(2,1)S(1)} %pad_maximum_fusion.own_ref), channel_id=1, source_target_pairs={{0,1},{1,0},{2,3},{3,2},{4,5},{5,4},{6,7},{7,6},{8,9},{9,8},{10,11... | collective-permute-start | bytes 1572872 | tf_op jit(solution)/shard_map/ppermute | solution.py:20
  38.3 0.9 collective-permute-done.9.l3
  39.2 0.6 collective-permute-done.6.other_ref
  39.8 14.8 %shard_map.88 = (bf16[32,8,1024]{2,1,0:T(8,128)(2,1)}, f32[32,128]{1,0:T(8,128)S(1)}) custom-call(s32[6]{0:T(128)S(1)} %reshape_reshape.4.sc, bf16[2,128,128,128]{3,2,1,0:T(8,128)(2,1)} %bitcast.32, bf16[4,8,8,1024]{3,2,1,0:T(8,128)(2,1)S(1)} %pad_maximum_fusion.own_ref, bf16[4,8,8,1024]{3,2,1,0:T(8,128)(2,1)S(1)} %collective-permute-done.6.other_ref, ...), custom_call_target="tpu_custom_call" | custom-call | flops 8589934592 | bytes 12582912 | tf_op jit(solution)/shard_map/pallas_call | solution.py:170
  54.6 2.9 %collective-permute-start.10 = (f32[32,128]{1,0:T(8,128)S(1)}, f32[32,128]{1,0:T(8,128)S(1)}, u32[]{:S(2)}, u32[]{:S(2)}) collective-permute-start(f32[32,128]{1,0:T(8,128)S(1)} %get-tuple-element.18), channel_id=1, source_target_pairs={{0,1},{1,0},{2,3},{3,2},{4,5},{5,4},{6,7},{7,6},{8,9},{9,8},{10,11... | collective-permute-start | bytes 49160 | tf_op jit(solution)/shard_map/ppermute | solution.py:20
  57.5 5.0 %all-to-all-start.1 = ((bf16[32,8,1024]{2,1,0:T(8,128)(2,1)}), bf16[32,8,1024]{2,1,0:T(8,128)(2,1)}, u32[]{:S(2)}, u32[]{:S(2)}) async-start(bf16[32,8,1024]{2,1,0:T(8,128)(2,1)} %get-tuple-element.19), calls=%async_computation.1 | async-start | bytes 1048576 | tf_op jit(solution)/shard_map/all_to_all | solution.py:272
  62.5 1.5 %collective-permute-start.11 = (f32[32,128]{1,0:T(8,128)S(1)}, f32[32,128]{1,0:T(8,128)S(1)}, u32[]{:S(2)}, u32[]{:S(2)}) collective-permute-start(f32[32,128]{1,0:T(8,128)S(1)} %add.165), channel_id=1, source_target_pairs={{0,2},{1,3},{2,4},{3,5},{4,6},{5,7},{6,0},{7,1},{8,10},{9,11},{10,... | collective-permute-start | bytes 49160 | tf_op jit(solution)/shard_map/ppermute | solution.py:16
  64.0 2.4 %collective-permute-start.12 = (f32[32,128]{1,0:T(8,128)S(1)}, f32[32,128]{1,0:T(8,128)S(1)}, u32[]{:S(2)}, u32[]{:S(2)}) collective-permute-start(f32[32,128]{1,0:T(8,128)S(1)} %add.165), channel_id=1, source_target_pairs={{0,4},{1,5},{2,6},{3,7},{4,0},{5,1},{6,2},{7,3},{8,12},{9,13},{10,... | collective-permute-start | bytes 49160 | tf_op jit(solution)/shard_map/ppermute | solution.py:16
  66.4 1.2 collective-permute-start.13
  67.5 4.4 %collective-permute-done.11 = f32[32,128]{1,0:T(8,128)S(1)} collective-permute-done((f32[32,128]{1,0:T(8,128)S(1)}, f32[32,128]{1,0:T(8,128)S(1)}, u32[]{:S(2)}, u32[]{:S(2)}) %collective-permute-start.11) | collective-permute-done | bytes 16416 | tf_op jit(solution)/shard_map/ppermute | solution.py:16
  71.9 0.7 collective-permute-done.12
  72.6 0.1 reshape.152
  72.8 0.1 eq.99
  72.9 0.1 slice_compare_fusion
  73.0 0.1 gt.31
  73.1 0.1 broadcast_in_dim.81
  73.2 0.1 gt.32
  73.3 0.8 all-to-all-done.1
  74.1 1.6 %convolution_convert_fusion.2 = bf16[16,1024]{1,0:T(8,128)(2,1)S(1)} fusion(bf16[1024,1024]{1,0:T(8,128)(2,1)S(1)} %copy-done, bf16[32,8,1024]{2,1,0:T(8,128)(2,1)} %all-to-all-done.1, s32[256]{0:T(256)S(1)} %and_select_fusion.3, f32[256]{0:T(256)S(1)} %eq.99, s32[16]{0:T(128)S(1)} %get-tuple-element.26, f32[16]{0:T(128)S(1)} %get-tuple-element.27, ...), kind=kOutput, calls=%fused_computation.4 | convolution fusion | flops 42000384 | bytes 2656640 | tf_op jit(solution)/shard_map/dot_general | solution.py:283
  75.7 1.2 fusion
  76.8 5.0 %all-to-all-start.2 = ((bf16[32,8,1024]{2,1,0:T(8,128)(2,1)}), bf16[32,8,1024]{2,1,0:T(8,128)(2,1)S(1)}, u32[]{:S(2)}, u32[]{:S(2)}) async-start(bf16[32,8,1024]{2,1,0:T(8,128)(2,1)} %fusion), calls=%async_computation.2 | async-start | bytes 1048576 | tf_op jit(solution)/shard_map/all_to_all | solution.py:285
  81.9 11.5 %all-to-all-done.2.got_ref = bf16[32,8,1024]{2,1,0:T(8,128)(2,1)S(1)} async-done(((bf16[32,8,1024]{2,1,0:T(8,128)(2,1)}), bf16[32,8,1024]{2,1,0:T(8,128)(2,1)S(1)}, u32[]{:S(2)}, u32[]{:S(2)}) %all-to-all-start.2) | async-done | bytes 524320 | tf_op jit(solution)/shard_map/all_to_all | solution.py:285
  93.4 13.1 %shard_map.89 = bf16[8,32,1024]{2,1,0:T(8,128)(2,1)} custom-call(bf16[2,128,128,128]{3,2,1,0:T(8,128)(2,1)} %bitcast.33, bf16[1024,1024]{1,0:T(8,128)(2,1)} %inverse_hbm.1, bf16[32,8,1024]{2,1,0:T(8,128)(2,1)S(1)} %all-to-all-done.2.got_ref, bf16[2,128,1024]{2,1,0:T(8,128)(2,1)S(1)} %shard_map.87.slab_ref.slabs_ref), custom_call_target="tpu_custom_call" | custom-call | flops 8589934592 | bytes 12582912 | tf_op jit(solution)/shard_map/pallas_call | solution.py:192
  106.6 3.9 %all-to-all-start.3 = ((bf16[8,32,1024]{2,1,0:T(8,128)(2,1)}), bf16[8,32,1024]{2,1,0:T(8,128)(2,1)S(1)}, u32[]{:S(2)}, u32[]{:S(2)}) async-start(bf16[8,32,1024]{2,1,0:T(8,128)(2,1)} %shard_map.89), calls=%async_computation.3 | async-start | bytes 1048576 | tf_op jit(solution)/shard_map/all_to_all | solution.py:297
  110.4 0.1 slice.42
  110.5 0.1 reshape.156
  110.7 0.1 eq.106
  110.8 0.1 slice_compare_fusion.1
  110.8 0.1 gt.34
  110.9 0.1 broadcast_in_dim.85
  111.0 0.1 gt.35
  111.2 0.1 collective-permute-start.14
  111.3 1.6 %collective-permute-start.15 = (bf16[1,4,1024]{2,1,0:T(4,128)(2,1)S(1)}, bf16[1,4,1024]{2,1,0:T(4,128)(2,1)S(1)}, u32[]{:S(2)}, u32[]{:S(2)}) collective-permute-start(bf16[1,4,1024]{2,1,0:T(4,128)(2,1)S(1)} %get-tuple-element.21), channel_id=1, source_target_pairs={{0,16},{8,24},{16,0},{24,8},{1,17},{9,25},{17,1},{25,9},{2,18},{10... | collective-permute-start | bytes 24584 | tf_op jit(solution)/shard_map/ppermute | solution.py:16
  112.9 1.4 %collective-permute-start.16 = (bf16[1,4,1024]{2,1,0:T(4,128)(2,1)S(1)}, bf16[1,4,1024]{2,1,0:T(4,128)(2,1)S(1)}, u32[]{:S(2)}, u32[]{:S(2)}) collective-permute-start(bf16[1,4,1024]{2,1,0:T(4,128)(2,1)S(1)} %get-tuple-element.20), channel_id=1, source_target_pairs={{0,24},{8,0},{16,8},{24,16},{1,25},{9,1},{17,9},{25,17},{2,26},{10... | collective-permute-start | bytes 24584 | tf_op jit(solution)/shard_map/ppermute | solution.py:16
  114.3 5.7 %all-to-all-done.3 = bf16[8,32,1024]{2,1,0:T(8,128)(2,1)S(1)} async-done(((bf16[8,32,1024]{2,1,0:T(8,128)(2,1)}), bf16[8,32,1024]{2,1,0:T(8,128)(2,1)S(1)}, u32[]{:S(2)}, u32[]{:S(2)}) %all-to-all-start.3) | async-done | bytes 524320 | tf_op jit(solution)/shard_map/all_to_all | solution.py:297
  119.9 0.9 fusion.1
  120.8 3.4 %all-to-all-start.4 = ((bf16[8,8,1024]{2,1,0:T(8,128)(2,1)}), bf16[8,8,1024]{2,1,0:T(8,128)(2,1)S(1)}, u32[]{:S(2)}, u32[]{:S(2)}) async-start(bf16[8,8,1024]{2,1,0:T(8,128)(2,1)} %fusion.1), calls=%async_computation.4 | async-start | bytes 262144 | tf_op jit(solution)/shard_map/all_to_all | solution.py:306
  124.3 0.6 reshape.155
  124.9 7.0 %all-to-all-done.4 = bf16[8,8,1024]{2,1,0:T(8,128)(2,1)S(1)} async-done(((bf16[8,8,1024]{2,1,0:T(8,128)(2,1)}), bf16[8,8,1024]{2,1,0:T(8,128)(2,1)S(1)}, u32[]{:S(2)}, u32[]{:S(2)}) %all-to-all-start.4) | async-done | bytes 131104 | tf_op jit(solution)/shard_map/all_to_all | solution.py:306
  131.9 0.6 add_convert_fusion
  (31 shorter events, 0.5 us)
Async XLA Ops:
  0.6 73.5 %copy-start = (bf16[1024,1024]{1,0:T(8,128)(2,1)S(1)}, bf16[1024,1024]{1,0:T(8,128)(2,1)}, u32[]{:S(2)}) copy-start(bf16[1024,1024]{1,0:T(8,128)(2,1)} %param.12) | copy-start | bytes 6291460
  2.4 23.2 %all-to-all-start = ((bf16[8,24,1024]{2,1,0:T(8,128)(2,1)}), bf16[8,24,1024]{2,1,0:T(8,128)(2,1)S(1)}, u32[]{:S(2)}, u32[]{:S(2)}) async-start(bf16[8,24,1024]{2,1,0:T(8,128)(2,1)} %broadcast_in_dim.75), calls=%async_computation | async-start | bytes 786432 | tf_op jit(solution)/shard_map/all_to_all | solution.py:250
  13.1 5.0 %collective-permute-start = (f32[4,128]{1,0:T(4,128)S(1)}, f32[4,128]{1,0:T(4,128)S(1)}, u32[]{:S(2)}, u32[]{:S(2)}) collective-permute-start(f32[4,128]{1,0:T(4,128)S(1)} %broadcast_select_fusion), channel_id=1, source_target_pairs={{0,8},{8,16},{16,24},{24,0},{1,9},{9,17},{17,25},{25,1},{2,10},{10... | collective-permute-start | bytes 6152 | tf_op jit(solution)/shard_map/ppermute | solution.py:16
  14.4 3.9 %collective-permute-start.1 = (f32[4,128]{1,0:T(4,128)S(1)}, f32[4,128]{1,0:T(4,128)S(1)}, u32[]{:S(2)}, u32[]{:S(2)}) collective-permute-start(f32[4,128]{1,0:T(4,128)S(1)} %broadcast_select_fusion), channel_id=1, source_target_pairs={{0,16},{8,24},{16,0},{24,8},{1,17},{9,25},{17,1},{25,9},{2,18},{10... | collective-permute-start | bytes 6152 | tf_op jit(solution)/shard_map/ppermute | solution.py:16
  17.0 2.7 %collective-permute-start.2 = (f32[4,128]{1,0:T(4,128)S(1)}, f32[4,128]{1,0:T(4,128)S(1)}, u32[]{:S(2)}, u32[]{:S(2)}) collective-permute-start(f32[4,128]{1,0:T(4,128)S(1)} %broadcast_select_fusion), channel_id=1, source_target_pairs={{0,24},{8,0},{16,8},{24,16},{1,25},{9,1},{17,9},{25,17},{2,26},{10... | collective-permute-start | bytes 6152 | tf_op jit(solution)/shard_map/ppermute | solution.py:16
  26.3 7.0 %collective-permute-start.3 = (bf16[8,8,1024]{2,1,0:T(8,128)(2,1)S(1)}, bf16[8,8,1024]{2,1,0:T(8,128)(2,1)S(1)}, u32[]{:S(2)}, u32[]{:S(2)}) collective-permute-start(bf16[8,8,1024]{2,1,0:T(8,128)(2,1)S(1)} %get-tuple-element.13), channel_id=1, source_target_pairs={{0,2},{1,3},{2,4},{3,5},{4,6},{5,7},{6,0},{7,1},{8,10},{9,11},{10,... | collective-permute-start | bytes 393224 | tf_op jit(solution)/shard_map/ppermute | solution.py:16
  27.6 7.4 %collective-permute-start.4 = (bf16[8,8,1024]{2,1,0:T(8,128)(2,1)S(1)}, bf16[8,8,1024]{2,1,0:T(8,128)(2,1)S(1)}, u32[]{:S(2)}, u32[]{:S(2)}) collective-permute-start(bf16[8,8,1024]{2,1,0:T(8,128)(2,1)S(1)} %get-tuple-element.13), channel_id=1, source_target_pairs={{0,6},{1,7},{2,0},{3,1},{4,2},{5,3},{6,4},{7,5},{8,14},{9,15},{10,... | collective-permute-start | bytes 393224 | tf_op jit(solution)/shard_map/ppermute | solution.py:16
  29.1 7.0 %collective-permute-start.5 = (bf16[8,8,1024]{2,1,0:T(8,128)(2,1)S(1)}, bf16[8,8,1024]{2,1,0:T(8,128)(2,1)S(1)}, u32[]{:S(2)}, u32[]{:S(2)}) collective-permute-start(bf16[8,8,1024]{2,1,0:T(8,128)(2,1)S(1)} %get-tuple-element.13), channel_id=1, source_target_pairs={{0,4},{1,5},{2,6},{3,7},{4,0},{5,1},{6,2},{7,3},{8,12},{9,13},{10,... | collective-permute-start | bytes 393224 | tf_op jit(solution)/shard_map/ppermute | solution.py:16
  30.6 7.7 %collective-permute-start.7 = (bf16[4,16,1024]{2,1,0:T(8,128)(2,1)S(1)}, bf16[4,16,1024]{2,1,0:T(8,128)(2,1)S(1)}, u32[]{:S(2)}, u32[]{:S(2)}) collective-permute-start(bf16[4,16,1024]{2,1,0:T(8,128)(2,1)S(1)} %get-tuple-element.15), channel_id=1, source_target_pairs={{0,8},{8,16},{16,24},{24,0},{1,9},{9,17},{17,25},{25,1},{2,10},{10... | collective-permute-start | bytes 393224 | tf_op jit(solution)/shard_map/ppermute | solution.py:16
  31.9 6.4 %collective-permute-start.8 = (bf16[4,16,1024]{2,1,0:T(8,128)(2,1)S(1)}, bf16[4,16,1024]{2,1,0:T(8,128)(2,1)S(1)}, u32[]{:S(2)}, u32[]{:S(2)}) collective-permute-start(bf16[4,16,1024]{2,1,0:T(8,128)(2,1)S(1)} %get-tuple-element.16), channel_id=1, source_target_pairs={{0,24},{8,0},{16,8},{24,16},{1,25},{9,1},{17,9},{25,17},{2,26},{10... | collective-permute-start | bytes 393224 | tf_op jit(solution)/shard_map/ppermute | solution.py:16
  33.4 5.8 %collective-permute-start.9 = (bf16[4,16,1024]{2,1,0:T(8,128)(2,1)S(1)}, bf16[4,16,1024]{2,1,0:T(8,128)(2,1)S(1)}, u32[]{:S(2)}, u32[]{:S(2)}) collective-permute-start(bf16[4,16,1024]{2,1,0:T(8,128)(2,1)S(1)} %get-tuple-element.17), channel_id=1, source_target_pairs={{0,16},{8,24},{16,0},{24,8},{1,17},{9,25},{17,1},{25,9},{2,18},{10... | collective-permute-start | bytes 393224 | tf_op jit(solution)/shard_map/ppermute | solution.py:16
  36.2 3.7 %collective-permute-start.6 = (bf16[4,8,8,1024]{3,2,1,0:T(8,128)(2,1)S(1)}, bf16[4,8,8,1024]{3,2,1,0:T(8,128)(2,1)S(1)}, u32[]{:S(2)}, u32[]{:S(2)}) collective-permute-start(bf16[4,8,8,1024]{3,2,1,0:T(8,128)(2,1)S(1)} %pad_maximum_fusion.own_ref), channel_id=1, source_target_pairs={{0,1},{1,0},{2,3},{3,2},{4,5},{5,4},{6,7},{7,6},{8,9},{9,8},{10,11... | collective-permute-start | bytes 1572872 | tf_op jit(solution)/shard_map/ppermute | solution.py:20
  54.6 7.9 %collective-permute-start.10 = (f32[32,128]{1,0:T(8,128)S(1)}, f32[32,128]{1,0:T(8,128)S(1)}, u32[]{:S(2)}, u32[]{:S(2)}) collective-permute-start(f32[32,128]{1,0:T(8,128)S(1)} %get-tuple-element.18), channel_id=1, source_target_pairs={{0,1},{1,0},{2,3},{3,2},{4,5},{5,4},{6,7},{7,6},{8,9},{9,8},{10,11... | collective-permute-start | bytes 49160 | tf_op jit(solution)/shard_map/ppermute | solution.py:20
  57.5 16.6 %all-to-all-start.1 = ((bf16[32,8,1024]{2,1,0:T(8,128)(2,1)}), bf16[32,8,1024]{2,1,0:T(8,128)(2,1)}, u32[]{:S(2)}, u32[]{:S(2)}) async-start(bf16[32,8,1024]{2,1,0:T(8,128)(2,1)} %get-tuple-element.19), calls=%async_computation.1 | async-start | bytes 1048576 | tf_op jit(solution)/shard_map/all_to_all | solution.py:272
  62.5 9.4 %collective-permute-start.11 = (f32[32,128]{1,0:T(8,128)S(1)}, f32[32,128]{1,0:T(8,128)S(1)}, u32[]{:S(2)}, u32[]{:S(2)}) collective-permute-start(f32[32,128]{1,0:T(8,128)S(1)} %add.165), channel_id=1, source_target_pairs={{0,2},{1,3},{2,4},{3,5},{4,6},{5,7},{6,0},{7,1},{8,10},{9,11},{10,... | collective-permute-start | bytes 49160 | tf_op jit(solution)/shard_map/ppermute | solution.py:16
  64.0 8.6 %collective-permute-start.12 = (f32[32,128]{1,0:T(8,128)S(1)}, f32[32,128]{1,0:T(8,128)S(1)}, u32[]{:S(2)}, u32[]{:S(2)}) collective-permute-start(f32[32,128]{1,0:T(8,128)S(1)} %add.165), channel_id=1, source_target_pairs={{0,4},{1,5},{2,6},{3,7},{4,0},{5,1},{6,2},{7,3},{8,12},{9,13},{10,... | collective-permute-start | bytes 49160 | tf_op jit(solution)/shard_map/ppermute | solution.py:16
  66.4 6.2 %collective-permute-start.13 = (f32[32,128]{1,0:T(8,128)S(1)}, f32[32,128]{1,0:T(8,128)S(1)}, u32[]{:S(2)}, u32[]{:S(2)}) collective-permute-start(f32[32,128]{1,0:T(8,128)S(1)} %add.165), channel_id=1, source_target_pairs={{0,6},{1,7},{2,0},{3,1},{4,2},{5,3},{6,4},{7,5},{8,14},{9,15},{10,... | collective-permute-start | bytes 49160 | tf_op jit(solution)/shard_map/ppermute | solution.py:16
  76.8 16.6 %all-to-all-start.2 = ((bf16[32,8,1024]{2,1,0:T(8,128)(2,1)}), bf16[32,8,1024]{2,1,0:T(8,128)(2,1)S(1)}, u32[]{:S(2)}, u32[]{:S(2)}) async-start(bf16[32,8,1024]{2,1,0:T(8,128)(2,1)} %fusion), calls=%async_computation.2 | async-start | bytes 1048576 | tf_op jit(solution)/shard_map/all_to_all | solution.py:285
  106.6 13.4 %all-to-all-start.3 = ((bf16[8,32,1024]{2,1,0:T(8,128)(2,1)}), bf16[8,32,1024]{2,1,0:T(8,128)(2,1)S(1)}, u32[]{:S(2)}, u32[]{:S(2)}) async-start(bf16[8,32,1024]{2,1,0:T(8,128)(2,1)} %shard_map.89), calls=%async_computation.3 | async-start | bytes 1048576 | tf_op jit(solution)/shard_map/all_to_all | solution.py:297
  111.2 13.0 %collective-permute-start.14 = (bf16[1,4,1024]{2,1,0:T(4,128)(2,1)S(1)}, bf16[1,4,1024]{2,1,0:T(4,128)(2,1)S(1)}, u32[]{:S(2)}, u32[]{:S(2)}) collective-permute-start(bf16[1,4,1024]{2,1,0:T(4,128)(2,1)S(1)} %get-tuple-element.22), channel_id=1, source_target_pairs={{0,8},{8,16},{16,24},{24,0},{1,9},{9,17},{17,25},{25,1},{2,10},{10... | collective-permute-start | bytes 24584 | tf_op jit(solution)/shard_map/ppermute | solution.py:16
  111.3 13.0 %collective-permute-start.15 = (bf16[1,4,1024]{2,1,0:T(4,128)(2,1)S(1)}, bf16[1,4,1024]{2,1,0:T(4,128)(2,1)S(1)}, u32[]{:S(2)}, u32[]{:S(2)}) collective-permute-start(bf16[1,4,1024]{2,1,0:T(4,128)(2,1)S(1)} %get-tuple-element.21), channel_id=1, source_target_pairs={{0,16},{8,24},{16,0},{24,8},{1,17},{9,25},{17,1},{25,9},{2,18},{10... | collective-permute-start | bytes 24584 | tf_op jit(solution)/shard_map/ppermute | solution.py:16
  112.9 11.4 %collective-permute-start.16 = (bf16[1,4,1024]{2,1,0:T(4,128)(2,1)S(1)}, bf16[1,4,1024]{2,1,0:T(4,128)(2,1)S(1)}, u32[]{:S(2)}, u32[]{:S(2)}) collective-permute-start(bf16[1,4,1024]{2,1,0:T(4,128)(2,1)S(1)} %get-tuple-element.20), channel_id=1, source_target_pairs={{0,24},{8,0},{16,8},{24,16},{1,25},{9,1},{17,9},{25,17},{2,26},{10... | collective-permute-start | bytes 24584 | tf_op jit(solution)/shard_map/ppermute | solution.py:16
  120.8 11.1 %all-to-all-start.4 = ((bf16[8,8,1024]{2,1,0:T(8,128)(2,1)}), bf16[8,8,1024]{2,1,0:T(8,128)(2,1)S(1)}, u32[]{:S(2)}, u32[]{:S(2)}) async-start(bf16[8,8,1024]{2,1,0:T(8,128)(2,1)} %fusion.1), calls=%async_computation.4 | async-start | bytes 262144 | tf_op jit(solution)/shard_map/all_to_all | solution.py:306
where the time goes:
time: 133 us
  starting transfers between devices  53 us (40%)
  waiting for transfers between devices  40.1 us (30%)
  Pallas kernels  28.6 us (22%)
  local copies, waits for them, and re-layouts  3.68 us (3%)
  matrix products  3.65 us (3%)
  other arithmetic  2.76 us (2%)
    ppermute x15, starting transfers between devices, rotated(): return lax.ppermute(x, axis, [(i, (i + distance) % n) for i in range(n)])  21.8 us
    pallas_call x1, Pallas kernels, first_products(): pl.pallas_call(first_kernel, grid_spec=pltpu.PrefetchScalarGridSpec(num_s...  14.8 us
    pallas_call x1, Pallas kernels, second_products(): pl.pallas_call(second_kernel, grid=(1,), in_specs=[*[pl.BlockSpec(memory_...  13.1 us
    all_to_all x1, waiting for transfers between devices, body(): got = lax.all_to_all(sent, ('ja', 'ka'), 0, 0, tiled=True)  11.5 us
    all_to_all x1, starting transfers between devices, body(): lax.all_to_all(jnp.broadcast_to(mine, (8, *mine.shape)), 'ia', 0, 0, tile...  9.01 us
    ppermute x15, waiting for transfers between devices, rotated(): return lax.ppermute(x, axis, [(i, (i + distance) % n) for i in range(n)])  8.7 us
    all_to_all x1, waiting for transfers between devices, body(): last = lax.all_to_all(partial.reshape(8, 8, r), 'ia', 0, 0, tiled=True)  6.95 us
    all_to_all x1, waiting for transfers between devices, body(): lax.all_to_all(jnp.broadcast_to(mine, (8, *mine.shape)), 'ia', 0, 0, tile...  5.81 us
  transfers between devices with their start and end apart: 22, of which 12 were waited for; matrix products, arithmetic and copies ran while one was open for 4% of the time, Pallas kernels for 0%

commit v1 on v0

--- a/solution.py
+++ b/solution.py
@@ -153,6 +153,7 @@
 
 
 PARAMS = pltpu.CompilerParams(vmem_limit_bytes=51 * 2**20)
+FIRST_PARAMS = pltpu.CompilerParams(vmem_limit_bytes=46 * 2**20)
 COST = pl.CostEstimate(flops=2 * 2 * 128**3 * 1024, bytes_accessed=12 * 2**20, transcendentals=0)
 
 
@@ -174,14 +175,14 @@
             grid=(2, BLK // CHUNK),
             in_specs=[
                 pl.BlockSpec((1, BLK, CHUNK, BLK), lambda s, q, sc: (s, 0, q, 0)),
-                *[whole(o) for o in others],
+                *[pl.BlockSpec(memory_space=pltpu.VMEM)] * len(others),
                 pl.BlockSpec((1, BLK, r), lambda s, q, sc: (s, 0, 0)),
             ],
             out_specs=[whole(o) for o in outs],
             scratch_shapes=scratch_for(r),
         ),
         out_shape=outs,
-        compiler_params=PARAMS,
+        compiler_params=FIRST_PARAMS,
         cost_estimate=COST,
     )(scalars, x, *others, slabs)
 
@@ -194,7 +195,7 @@
         grid=(1,),
         in_specs=[
             *[pl.BlockSpec(memory_space=pltpu.HBM)] * 2,
-            *[whole(o) for o in others],
+            *[pl.BlockSpec(memory_space=pltpu.VMEM)] * len(others),
         ],
         out_specs=whole(out),
         scratch_shapes=[

time: 133 us -> 133 us (level)
  no operation moved by 1% of the time
where the time goes in v1:
time: 133 us
  starting transfers between devices  53 us (40%)
  waiting for transfers between devices  40.1 us (30%)
  Pallas kernels  28.6 us (22%)
  local copies, waits for them, and re-layouts  3.68 us (3%)
  matrix products  3.65 us (3%)
  other arithmetic  2.76 us (2%)
    ppermute x15, starting transfers between devices, rotated(): return lax.ppermute(x, axis, [(i, (i + distance) % n) for i in range(n)])  21.8 us
    pallas_call x1, Pallas kernels, first_products(): pl.pallas_call(first_kernel, grid_spec=pltpu.PrefetchScalarGridSpec(num_s...  14.8 us
    pallas_call x1, Pallas kernels, second_products(): pl.pallas_call(second_kernel, grid=(1,), in_specs=[*[pl.BlockSpec(memory_...  13.1 us
    all_to_all x1, waiting for transfers between devices, body(): got = lax.all_to_all(sent, ('ja', 'ka'), 0, 0, tiled=True)  11.5 us
    all_to_all x1, starting transfers between devices, body(): lax.all_to_all(jnp.broadcast_to(mine, (8, *mine.shape)), 'ia', 0, 0, tile...  9.01 us
    ppermute x15, waiting for transfers between devices, rotated(): return lax.ppermute(x, axis, [(i, (i + distance) % n) for i in range(n)])  8.7 us
    all_to_all x1, waiting for transfers between devices, body(): last = lax.all_to_all(partial.reshape(8, 8, r), 'ia', 0, 0, tiled=True)  6.95 us
    all_to_all x1, waiting for transfers between devices, body(): lax.all_to_all(jnp.broadcast_to(mine, (8, *mine.shape)), 'ia', 0, 0, tile...  5.81 us
  transfers between devices with their start and end apart: 22, of which 12 were waited for; matrix products, arithmetic and copies ran while one was open for 4% of the time, Pallas kernels for 0%

profile of v1, /device:TPU:1, one launch (start us, length us, event | category | flops | bytes accessed | tf_op | source)
XLA Modules:
  0.0 132.5 jit_solution(9849648454889171452)
XLA Ops:
  0.6 0.9 pad_maximum_fusion.1
  1.6 0.8 broadcast_in_dim.75
  2.4 9.0 %all-to-all-start = ((bf16[8,24,1024]{2,1,0:T(8,128)(2,1)}), bf16[8,24,1024]{2,1,0:T(8,128)(2,1)S(1)}, u32[]{:S(2)}, u32[]{:S(2)}) async-start(bf16[8,24,1024]{2,1,0:T(8,128)(2,1)} %broadcast_in_dim.75), calls=%async_computation | async-start | bytes 786432 | tf_op jit(solution)/shard_map/all_to_all | solution.py:251
  11.4 0.8 copy.10
  12.2 0.1 reshape_reshape.4.sc
  12.2 0.7 add_convert_fusion.1
  13.0 0.1 broadcast_select_fusion
  13.1 1.3 collective-permute-start
  14.4 2.6 %collective-permute-start.1 = (f32[4,128]{1,0:T(4,128)S(1)}, f32[4,128]{1,0:T(4,128)S(1)}, u32[]{:S(2)}, u32[]{:S(2)}) collective-permute-start(f32[4,128]{1,0:T(4,128)S(1)} %broadcast_select_fusion), channel_id=1, source_target_pairs={{0,16},{8,24},{16,0},{24,8},{1,17},{9,25},{17,1},{25,9},{2,18},{10... | collective-permute-start | bytes 6152 | tf_op jit(solution)/shard_map/ppermute | solution.py:16
  17.0 1.1 collective-permute-start.2
  18.0 0.2 collective-permute-done.1
  18.3 1.4 %collective-permute-done.2 = f32[4,128]{1,0:T(4,128)S(1)} collective-permute-done((f32[4,128]{1,0:T(4,128)S(1)}, f32[4,128]{1,0:T(4,128)S(1)}, u32[]{:S(2)}, u32[]{:S(2)}) %collective-permute-start.2) | collective-permute-done | bytes 2080 | tf_op jit(solution)/shard_map/ppermute | solution.py:16
  19.7 0.1 add_add_fusion.1.tags_ref
  19.8 5.8 %all-to-all-done.along_ref = bf16[8,24,1024]{2,1,0:T(8,128)(2,1)S(1)} async-done(((bf16[8,24,1024]{2,1,0:T(8,128)(2,1)}), bf16[8,24,1024]{2,1,0:T(8,128)(2,1)S(1)}, u32[]{:S(2)}, u32[]{:S(2)}) %all-to-all-start) | async-done | bytes 393248 | tf_op jit(solution)/shard_map/all_to_all | solution.py:251
  25.6 0.1 slice_convert_fusion
  25.7 0.1 convert_element_type.90.sc
  25.7 0.6 shard_map.86
  26.3 1.3 collective-permute-start.3
  27.6 1.5 %collective-permute-start.4 = (bf16[8,8,1024]{2,1,0:T(8,128)(2,1)S(1)}, bf16[8,8,1024]{2,1,0:T(8,128)(2,1)S(1)}, u32[]{:S(2)}, u32[]{:S(2)}) collective-permute-start(bf16[8,8,1024]{2,1,0:T(8,128)(2,1)S(1)} %get-tuple-element.13), channel_id=1, source_target_pairs={{0,6},{1,7},{2,0},{3,1},{4,2},{5,3},{6,4},{7,5},{8,14},{9,15},{10,... | collective-permute-start | bytes 393224 | tf_op jit(solution)/shard_map/ppermute | solution.py:16
  29.1 1.5 %collective-permute-start.5 = (bf16[8,8,1024]{2,1,0:T(8,128)(2,1)S(1)}, bf16[8,8,1024]{2,1,0:T(8,128)(2,1)S(1)}, u32[]{:S(2)}, u32[]{:S(2)}) collective-permute-start(bf16[8,8,1024]{2,1,0:T(8,128)(2,1)S(1)} %get-tuple-element.13), channel_id=1, source_target_pairs={{0,4},{1,5},{2,6},{3,7},{4,0},{5,1},{6,2},{7,3},{8,12},{9,13},{10,... | collective-permute-start | bytes 393224 | tf_op jit(solution)/shard_map/ppermute | solution.py:16
  30.6 1.3 collective-permute-start.7
  31.9 1.4 %collective-permute-start.8 = (bf16[4,16,1024]{2,1,0:T(8,128)(2,1)S(1)}, bf16[4,16,1024]{2,1,0:T(8,128)(2,1)S(1)}, u32[]{:S(2)}, u32[]{:S(2)}) collective-permute-start(bf16[4,16,1024]{2,1,0:T(8,128)(2,1)S(1)} %get-tuple-element.16), channel_id=1, source_target_pairs={{0,24},{8,0},{16,8},{24,16},{1,25},{9,1},{17,9},{25,17},{2,26},{10... | collective-permute-start | bytes 393224 | tf_op jit(solution)/shard_map/ppermute | solution.py:16
  33.4 1.6 %collective-permute-start.9 = (bf16[4,16,1024]{2,1,0:T(8,128)(2,1)S(1)}, bf16[4,16,1024]{2,1,0:T(8,128)(2,1)S(1)}, u32[]{:S(2)}, u32[]{:S(2)}) collective-permute-start(bf16[4,16,1024]{2,1,0:T(8,128)(2,1)S(1)} %get-tuple-element.17), channel_id=1, source_target_pairs={{0,16},{8,24},{16,0},{24,8},{1,17},{9,25},{17,1},{25,9},{2,18},{10... | collective-permute-start | bytes 393224 | tf_op jit(solution)/shard_map/ppermute | solution.py:16
  35.0 1.1 collective-permute-done.5
  36.2 2.1 %collective-permute-start.6 = (bf16[4,8,8,1024]{3,2,1,0:T(8,128)(2,1)S(1)}, bf16[4,8,8,1024]{3,2,1,0:T(8,128)(2,1)S(1)}, u32[]{:S(2)}, u32[]{:S(2)}) collective-permute-start(bf16[4,8,8,1024]{3,2,1,0:T(8,128)(2,1)S(1)} %pad_maximum_fusion.own_ref), channel_id=1, source_target_pairs={{0,1},{1,0},{2,3},{3,2},{4,5},{5,4},{6,7},{7,6},{8,9},{9,8},{10,11... | collective-permute-start | bytes 1572872 | tf_op jit(solution)/shard_map/ppermute | solution.py:20
  38.3 0.9 collective-permute-done.9.l3
  39.2 0.6 collective-permute-done.6.other_ref
  39.8 14.8 %shard_map.88 = (bf16[32,8,1024]{2,1,0:T(8,128)(2,1)}, f32[32,128]{1,0:T(8,128)S(1)}) custom-call(s32[6]{0:T(128)S(1)} %reshape_reshape.4.sc, bf16[2,128,128,128]{3,2,1,0:T(8,128)(2,1)} %bitcast.32, bf16[4,8,8,1024]{3,2,1,0:T(8,128)(2,1)S(1)} %pad_maximum_fusion.own_ref, bf16[4,8,8,1024]{3,2,1,0:T(8,128)(2,1)S(1)} %collective-permute-done.6.other_ref, ...), custom_call_target="tpu_custom_call" | custom-call | flops 8589934592 | bytes 12582912 | tf_op jit(solution)/shard_map/pallas_call | solution.py:171
  54.6 2.9 %collective-permute-start.10 = (f32[32,128]{1,0:T(8,128)S(1)}, f32[32,128]{1,0:T(8,128)S(1)}, u32[]{:S(2)}, u32[]{:S(2)}) collective-permute-start(f32[32,128]{1,0:T(8,128)S(1)} %get-tuple-element.18), channel_id=1, source_target_pairs={{0,1},{1,0},{2,3},{3,2},{4,5},{5,4},{6,7},{7,6},{8,9},{9,8},{10,11... | collective-permute-start | bytes 49160 | tf_op jit(solution)/shard_map/ppermute | solution.py:20
  57.5 5.0 %all-to-all-start.1 = ((bf16[32,8,1024]{2,1,0:T(8,128)(2,1)}), bf16[32,8,1024]{2,1,0:T(8,128)(2,1)}, u32[]{:S(2)}, u32[]{:S(2)}) async-start(bf16[32,8,1024]{2,1,0:T(8,128)(2,1)} %get-tuple-element.19), calls=%async_computation.1 | async-start | bytes 1048576 | tf_op jit(solution)/shard_map/all_to_all | solution.py:273
  62.5 1.5 %collective-permute-start.11 = (f32[32,128]{1,0:T(8,128)S(1)}, f32[32,128]{1,0:T(8,128)S(1)}, u32[]{:S(2)}, u32[]{:S(2)}) collective-permute-start(f32[32,128]{1,0:T(8,128)S(1)} %add.165), channel_id=1, source_target_pairs={{0,2},{1,3},{2,4},{3,5},{4,6},{5,7},{6,0},{7,1},{8,10},{9,11},{10,... | collective-permute-start | bytes 49160 | tf_op jit(solution)/shard_map/ppermute | solution.py:16
  64.0 2.4 %collective-permute-start.12 = (f32[32,128]{1,0:T(8,128)S(1)}, f32[32,128]{1,0:T(8,128)S(1)}, u32[]{:S(2)}, u32[]{:S(2)}) collective-permute-start(f32[32,128]{1,0:T(8,128)S(1)} %add.165), channel_id=1, source_target_pairs={{0,4},{1,5},{2,6},{3,7},{4,0},{5,1},{6,2},{7,3},{8,12},{9,13},{10,... | collective-permute-start | bytes 49160 | tf_op jit(solution)/shard_map/ppermute | solution.py:16
  66.4 1.2 collective-permute-start.13
  67.5 4.4 %collective-permute-done.11 = f32[32,128]{1,0:T(8,128)S(1)} collective-permute-done((f32[32,128]{1,0:T(8,128)S(1)}, f32[32,128]{1,0:T(8,128)S(1)}, u32[]{:S(2)}, u32[]{:S(2)}) %collective-permute-start.11) | collective-permute-done | bytes 16416 | tf_op jit(solution)/shard_map/ppermute | solution.py:16
  71.9 0.7 collective-permute-done.12
  72.6 0.1 reshape.152
  72.8 0.1 eq.99
  72.9 0.1 slice_compare_fusion
  73.0 0.1 gt.31
  73.1 0.1 broadcast_in_dim.81
  73.2 0.1 gt.32
  73.3 0.8 all-to-all-done.1
  74.1 1.6 %convolution_convert_fusion.2 = bf16[16,1024]{1,0:T(8,128)(2,1)S(1)} fusion(bf16[1024,1024]{1,0:T(8,128)(2,1)S(1)} %copy-done, bf16[32,8,1024]{2,1,0:T(8,128)(2,1)} %all-to-all-done.1, s32[256]{0:T(256)S(1)} %and_select_fusion.3, f32[256]{0:T(256)S(1)} %eq.99, s32[16]{0:T(128)S(1)} %get-tuple-element.26, f32[16]{0:T(128)S(1)} %get-tuple-element.27, ...), kind=kOutput, calls=%fused_computation.4 | convolution fusion | flops 42000384 | bytes 2656640 | tf_op jit(solution)/shard_map/dot_general | solution.py:284
  75.7 1.2 fusion
  76.8 5.0 %all-to-all-start.2 = ((bf16[32,8,1024]{2,1,0:T(8,128)(2,1)}), bf16[32,8,1024]{2,1,0:T(8,128)(2,1)S(1)}, u32[]{:S(2)}, u32[]{:S(2)}) async-start(bf16[32,8,1024]{2,1,0:T(8,128)(2,1)} %fusion), calls=%async_computation.2 | async-start | bytes 1048576 | tf_op jit(solution)/shard_map/all_to_all | solution.py:286
  81.9 11.5 %all-to-all-done.2.got_ref = bf16[32,8,1024]{2,1,0:T(8,128)(2,1)S(1)} async-done(((bf16[32,8,1024]{2,1,0:T(8,128)(2,1)}), bf16[32,8,1024]{2,1,0:T(8,128)(2,1)S(1)}, u32[]{:S(2)}, u32[]{:S(2)}) %all-to-all-start.2) | async-done | bytes 524320 | tf_op jit(solution)/shard_map/all_to_all | solution.py:286
  93.4 13.1 %shard_map.89 = bf16[8,32,1024]{2,1,0:T(8,128)(2,1)} custom-call(bf16[2,128,128,128]{3,2,1,0:T(8,128)(2,1)} %bitcast.33, bf16[1024,1024]{1,0:T(8,128)(2,1)} %inverse_hbm.1, bf16[32,8,1024]{2,1,0:T(8,128)(2,1)S(1)} %all-to-all-done.2.got_ref, bf16[2,128,1024]{2,1,0:T(8,128)(2,1)S(1)} %shard_map.87.slab_ref.slabs_ref), custom_call_target="tpu_custom_call" | custom-call | flops 8589934592 | bytes 12582912 | tf_op jit(solution)/shard_map/pallas_call | solution.py:193
  106.6 3.9 %all-to-all-start.3 = ((bf16[8,32,1024]{2,1,0:T(8,128)(2,1)}), bf16[8,32,1024]{2,1,0:T(8,128)(2,1)S(1)}, u32[]{:S(2)}, u32[]{:S(2)}) async-start(bf16[8,32,1024]{2,1,0:T(8,128)(2,1)} %shard_map.89), calls=%async_computation.3 | async-start | bytes 1048576 | tf_op jit(solution)/shard_map/all_to_all | solution.py:298
  110.4 0.1 slice.42
  110.5 0.1 reshape.156
  110.7 0.1 eq.106
  110.8 0.1 slice_compare_fusion.1
  110.8 0.1 gt.34
  110.9 0.1 broadcast_in_dim.85
  111.0 0.1 gt.35
  111.2 0.1 collective-permute-start.14
  111.3 1.6 %collective-permute-start.15 = (bf16[1,4,1024]{2,1,0:T(4,128)(2,1)S(1)}, bf16[1,4,1024]{2,1,0:T(4,128)(2,1)S(1)}, u32[]{:S(2)}, u32[]{:S(2)}) collective-permute-start(bf16[1,4,1024]{2,1,0:T(4,128)(2,1)S(1)} %get-tuple-element.21), channel_id=1, source_target_pairs={{0,16},{8,24},{16,0},{24,8},{1,17},{9,25},{17,1},{25,9},{2,18},{10... | collective-permute-start | bytes 24584 | tf_op jit(solution)/shard_map/ppermute | solution.py:16
  112.9 1.4 %collective-permute-start.16 = (bf16[1,4,1024]{2,1,0:T(4,128)(2,1)S(1)}, bf16[1,4,1024]{2,1,0:T(4,128)(2,1)S(1)}, u32[]{:S(2)}, u32[]{:S(2)}) collective-permute-start(bf16[1,4,1024]{2,1,0:T(4,128)(2,1)S(1)} %get-tuple-element.20), channel_id=1, source_target_pairs={{0,24},{8,0},{16,8},{24,16},{1,25},{9,1},{17,9},{25,17},{2,26},{10... | collective-permute-start | bytes 24584 | tf_op jit(solution)/shard_map/ppermute | solution.py:16
  114.3 5.7 %all-to-all-done.3 = bf16[8,32,1024]{2,1,0:T(8,128)(2,1)S(1)} async-done(((bf16[8,32,1024]{2,1,0:T(8,128)(2,1)}), bf16[8,32,1024]{2,1,0:T(8,128)(2,1)S(1)}, u32[]{:S(2)}, u32[]{:S(2)}) %all-to-all-start.3) | async-done | bytes 524320 | tf_op jit(solution)/shard_map/all_to_all | solution.py:298
  119.9 0.9 fusion.1
  120.8 3.4 %all-to-all-start.4 = ((bf16[8,8,1024]{2,1,0:T(8,128)(2,1)}), bf16[8,8,1024]{2,1,0:T(8,128)(2,1)S(1)}, u32[]{:S(2)}, u32[]{:S(2)}) async-start(bf16[8,8,1024]{2,1,0:T(8,128)(2,1)} %fusion.1), calls=%async_computation.4 | async-start | bytes 262144 | tf_op jit(solution)/shard_map/all_to_all | solution.py:307
  124.3 0.6 reshape.155
  124.9 7.0 %all-to-all-done.4 = bf16[8,8,1024]{2,1,0:T(8,128)(2,1)S(1)} async-done(((bf16[8,8,1024]{2,1,0:T(8,128)(2,1)}), bf16[8,8,1024]{2,1,0:T(8,128)(2,1)S(1)}, u32[]{:S(2)}, u32[]{:S(2)}) %all-to-all-start.4) | async-done | bytes 131104 | tf_op jit(solution)/shard_map/all_to_all | solution.py:307
  131.9 0.6 add_convert_fusion
  (31 shorter events, 0.5 us)
Async XLA Ops:
  0.6 73.5 %copy-start = (bf16[1024,1024]{1,0:T(8,128)(2,1)S(1)}, bf16[1024,1024]{1,0:T(8,128)(2,1)}, u32[]{:S(2)}) copy-start(bf16[1024,1024]{1,0:T(8,128)(2,1)} %param.12) | copy-start | bytes 6291460
  2.4 23.2 %all-to-all-start = ((bf16[8,24,1024]{2,1,0:T(8,128)(2,1)}), bf16[8,24,1024]{2,1,0:T(8,128)(2,1)S(1)}, u32[]{:S(2)}, u32[]{:S(2)}) async-start(bf16[8,24,1024]{2,1,0:T(8,128)(2,1)} %broadcast_in_dim.75), calls=%async_computation | async-start | bytes 786432 | tf_op jit(solution)/shard_map/all_to_all | solution.py:251
  13.1 5.0 %collective-permute-start = (f32[4,128]{1,0:T(4,128)S(1)}, f32[4,128]{1,0:T(4,128)S(1)}, u32[]{:S(2)}, u32[]{:S(2)}) collective-permute-start(f32[4,128]{1,0:T(4,128)S(1)} %broadcast_select_fusion), channel_id=1, source_target_pairs={{0,8},{8,16},{16,24},{24,0},{1,9},{9,17},{17,25},{25,1},{2,10},{10... | collective-permute-start | bytes 6152 | tf_op jit(solution)/shard_map/ppermute | solution.py:16
  14.4 3.9 %collective-permute-start.1 = (f32[4,128]{1,0:T(4,128)S(1)}, f32[4,128]{1,0:T(4,128)S(1)}, u32[]{:S(2)}, u32[]{:S(2)}) collective-permute-start(f32[4,128]{1,0:T(4,128)S(1)} %broadcast_select_fusion), channel_id=1, source_target_pairs={{0,16},{8,24},{16,0},{24,8},{1,17},{9,25},{17,1},{25,9},{2,18},{10... | collective-permute-start | bytes 6152 | tf_op jit(solution)/shard_map/ppermute | solution.py:16
  17.0 2.7 %collective-permute-start.2 = (f32[4,128]{1,0:T(4,128)S(1)}, f32[4,128]{1,0:T(4,128)S(1)}, u32[]{:S(2)}, u32[]{:S(2)}) collective-permute-start(f32[4,128]{1,0:T(4,128)S(1)} %broadcast_select_fusion), channel_id=1, source_target_pairs={{0,24},{8,0},{16,8},{24,16},{1,25},{9,1},{17,9},{25,17},{2,26},{10... | collective-permute-start | bytes 6152 | tf_op jit(solution)/shard_map/ppermute | solution.py:16
  26.3 7.0 %collective-permute-start.3 = (bf16[8,8,1024]{2,1,0:T(8,128)(2,1)S(1)}, bf16[8,8,1024]{2,1,0:T(8,128)(2,1)S(1)}, u32[]{:S(2)}, u32[]{:S(2)}) collective-permute-start(bf16[8,8,1024]{2,1,0:T(8,128)(2,1)S(1)} %get-tuple-element.13), channel_id=1, source_target_pairs={{0,2},{1,3},{2,4},{3,5},{4,6},{5,7},{6,0},{7,1},{8,10},{9,11},{10,... | collective-permute-start | bytes 393224 | tf_op jit(solution)/shard_map/ppermute | solution.py:16
  27.6 7.4 %collective-permute-start.4 = (bf16[8,8,1024]{2,1,0:T(8,128)(2,1)S(1)}, bf16[8,8,1024]{2,1,0:T(8,128)(2,1)S(1)}, u32[]{:S(2)}, u32[]{:S(2)}) collective-permute-start(bf16[8,8,1024]{2,1,0:T(8,128)(2,1)S(1)} %get-tuple-element.13), channel_id=1, source_target_pairs={{0,6},{1,7},{2,0},{3,1},{4,2},{5,3},{6,4},{7,5},{8,14},{9,15},{10,... | collective-permute-start | bytes 393224 | tf_op jit(solution)/shard_map/ppermute | solution.py:16
  29.1 7.0 %collective-permute-start.5 = (bf16[8,8,1024]{2,1,0:T(8,128)(2,1)S(1)}, bf16[8,8,1024]{2,1,0:T(8,128)(2,1)S(1)}, u32[]{:S(2)}, u32[]{:S(2)}) collective-permute-start(bf16[8,8,1024]{2,1,0:T(8,128)(2,1)S(1)} %get-tuple-element.13), channel_id=1, source_target_pairs={{0,4},{1,5},{2,6},{3,7},{4,0},{5,1},{6,2},{7,3},{8,12},{9,13},{10,... | collective-permute-start | bytes 393224 | tf_op jit(solution)/shard_map/ppermute | solution.py:16
  30.6 7.7 %collective-permute-start.7 = (bf16[4,16,1024]{2,1,0:T(8,128)(2,1)S(1)}, bf16[4,16,1024]{2,1,0:T(8,128)(2,1)S(1)}, u32[]{:S(2)}, u32[]{:S(2)}) collective-permute-start(bf16[4,16,1024]{2,1,0:T(8,128)(2,1)S(1)} %get-tuple-element.15), channel_id=1, source_target_pairs={{0,8},{8,16},{16,24},{24,0},{1,9},{9,17},{17,25},{25,1},{2,10},{10... | collective-permute-start | bytes 393224 | tf_op jit(solution)/shard_map/ppermute | solution.py:16
  31.9 6.4 %collective-permute-start.8 = (bf16[4,16,1024]{2,1,0:T(8,128)(2,1)S(1)}, bf16[4,16,1024]{2,1,0:T(8,128)(2,1)S(1)}, u32[]{:S(2)}, u32[]{:S(2)}) collective-permute-start(bf16[4,16,1024]{2,1,0:T(8,128)(2,1)S(1)} %get-tuple-element.16), channel_id=1, source_target_pairs={{0,24},{8,0},{16,8},{24,16},{1,25},{9,1},{17,9},{25,17},{2,26},{10... | collective-permute-start | bytes 393224 | tf_op jit(solution)/shard_map/ppermute | solution.py:16
  33.4 5.8 %collective-permute-start.9 = (bf16[4,16,1024]{2,1,0:T(8,128)(2,1)S(1)}, bf16[4,16,1024]{2,1,0:T(8,128)(2,1)S(1)}, u32[]{:S(2)}, u32[]{:S(2)}) collective-permute-start(bf16[4,16,1024]{2,1,0:T(8,128)(2,1)S(1)} %get-tuple-element.17), channel_id=1, source_target_pairs={{0,16},{8,24},{16,0},{24,8},{1,17},{9,25},{17,1},{25,9},{2,18},{10... | collective-permute-start | bytes 393224 | tf_op jit(solution)/shard_map/ppermute | solution.py:16
  36.2 3.7 %collective-permute-start.6 = (bf16[4,8,8,1024]{3,2,1,0:T(8,128)(2,1)S(1)}, bf16[4,8,8,1024]{3,2,1,0:T(8,128)(2,1)S(1)}, u32[]{:S(2)}, u32[]{:S(2)}) collective-permute-start(bf16[4,8,8,1024]{3,2,1,0:T(8,128)(2,1)S(1)} %pad_maximum_fusion.own_ref), channel_id=1, source_target_pairs={{0,1},{1,0},{2,3},{3,2},{4,5},{5,4},{6,7},{7,6},{8,9},{9,8},{10,11... | collective-permute-start | bytes 1572872 | tf_op jit(solution)/shard_map/ppermute | solution.py:20
  54.6 7.9 %collective-permute-start.10 = (f32[32,128]{1,0:T(8,128)S(1)}, f32[32,128]{1,0:T(8,128)S(1)}, u32[]{:S(2)}, u32[]{:S(2)}) collective-permute-start(f32[32,128]{1,0:T(8,128)S(1)} %get-tuple-element.18), channel_id=1, source_target_pairs={{0,1},{1,0},{2,3},{3,2},{4,5},{5,4},{6,7},{7,6},{8,9},{9,8},{10,11... | collective-permute-start | bytes 49160 | tf_op jit(solution)/shard_map/ppermute | solution.py:20
  57.5 16.6 %all-to-all-start.1 = ((bf16[32,8,1024]{2,1,0:T(8,128)(2,1)}), bf16[32,8,1024]{2,1,0:T(8,128)(2,1)}, u32[]{:S(2)}, u32[]{:S(2)}) async-start(bf16[32,8,1024]{2,1,0:T(8,128)(2,1)} %get-tuple-element.19), calls=%async_computation.1 | async-start | bytes 1048576 | tf_op jit(solution)/shard_map/all_to_all | solution.py:273
  62.5 9.4 %collective-permute-start.11 = (f32[32,128]{1,0:T(8,128)S(1)}, f32[32,128]{1,0:T(8,128)S(1)}, u32[]{:S(2)}, u32[]{:S(2)}) collective-permute-start(f32[32,128]{1,0:T(8,128)S(1)} %add.165), channel_id=1, source_target_pairs={{0,2},{1,3},{2,4},{3,5},{4,6},{5,7},{6,0},{7,1},{8,10},{9,11},{10,... | collective-permute-start | bytes 49160 | tf_op jit(solution)/shard_map/ppermute | solution.py:16
  64.0 8.6 %collective-permute-start.12 = (f32[32,128]{1,0:T(8,128)S(1)}, f32[32,128]{1,0:T(8,128)S(1)}, u32[]{:S(2)}, u32[]{:S(2)}) collective-permute-start(f32[32,128]{1,0:T(8,128)S(1)} %add.165), channel_id=1, source_target_pairs={{0,4},{1,5},{2,6},{3,7},{4,0},{5,1},{6,2},{7,3},{8,12},{9,13},{10,... | collective-permute-start | bytes 49160 | tf_op jit(solution)/shard_map/ppermute | solution.py:16
  66.4 6.2 %collective-permute-start.13 = (f32[32,128]{1,0:T(8,128)S(1)}, f32[32,128]{1,0:T(8,128)S(1)}, u32[]{:S(2)}, u32[]{:S(2)}) collective-permute-start(f32[32,128]{1,0:T(8,128)S(1)} %add.165), channel_id=1, source_target_pairs={{0,6},{1,7},{2,0},{3,1},{4,2},{5,3},{6,4},{7,5},{8,14},{9,15},{10,... | collective-permute-start | bytes 49160 | tf_op jit(solution)/shard_map/ppermute | solution.py:16
  76.8 16.6 %all-to-all-start.2 = ((bf16[32,8,1024]{2,1,0:T(8,128)(2,1)}), bf16[32,8,1024]{2,1,0:T(8,128)(2,1)S(1)}, u32[]{:S(2)}, u32[]{:S(2)}) async-start(bf16[32,8,1024]{2,1,0:T(8,128)(2,1)} %fusion), calls=%async_computation.2 | async-start | bytes 1048576 | tf_op jit(solution)/shard_map/all_to_all | solution.py:286
  106.6 13.4 %all-to-all-start.3 = ((bf16[8,32,1024]{2,1,0:T(8,128)(2,1)}), bf16[8,32,1024]{2,1,0:T(8,128)(2,1)S(1)}, u32[]{:S(2)}, u32[]{:S(2)}) async-start(bf16[8,32,1024]{2,1,0:T(8,128)(2,1)} %shard_map.89), calls=%async_computation.3 | async-start | bytes 1048576 | tf_op jit(solution)/shard_map/all_to_all | solution.py:298
  111.2 13.0 %collective-permute-start.14 = (bf16[1,4,1024]{2,1,0:T(4,128)(2,1)S(1)}, bf16[1,4,1024]{2,1,0:T(4,128)(2,1)S(1)}, u32[]{:S(2)}, u32[]{:S(2)}) collective-permute-start(bf16[1,4,1024]{2,1,0:T(4,128)(2,1)S(1)} %get-tuple-element.22), channel_id=1, source_target_pairs={{0,8},{8,16},{16,24},{24,0},{1,9},{9,17},{17,25},{25,1},{2,10},{10... | collective-permute-start | bytes 24584 | tf_op jit(solution)/shard_map/ppermute | solution.py:16
  111.3 13.0 %collective-permute-start.15 = (bf16[1,4,1024]{2,1,0:T(4,128)(2,1)S(1)}, bf16[1,4,1024]{2,1,0:T(4,128)(2,1)S(1)}, u32[]{:S(2)}, u32[]{:S(2)}) collective-permute-start(bf16[1,4,1024]{2,1,0:T(4,128)(2,1)S(1)} %get-tuple-element.21), channel_id=1, source_target_pairs={{0,16},{8,24},{16,0},{24,8},{1,17},{9,25},{17,1},{25,9},{2,18},{10... | collective-permute-start | bytes 24584 | tf_op jit(solution)/shard_map/ppermute | solution.py:16
  112.9 11.4 %collective-permute-start.16 = (bf16[1,4,1024]{2,1,0:T(4,128)(2,1)S(1)}, bf16[1,4,1024]{2,1,0:T(4,128)(2,1)S(1)}, u32[]{:S(2)}, u32[]{:S(2)}) collective-permute-start(bf16[1,4,1024]{2,1,0:T(4,128)(2,1)S(1)} %get-tuple-element.20), channel_id=1, source_target_pairs={{0,24},{8,0},{16,8},{24,16},{1,25},{9,1},{17,9},{25,17},{2,26},{10... | collective-permute-start | bytes 24584 | tf_op jit(solution)/shard_map/ppermute | solution.py:16
  120.8 11.1 %all-to-all-start.4 = ((bf16[8,8,1024]{2,1,0:T(8,128)(2,1)}), bf16[8,8,1024]{2,1,0:T(8,128)(2,1)S(1)}, u32[]{:S(2)}, u32[]{:S(2)}) async-start(bf16[8,8,1024]{2,1,0:T(8,128)(2,1)} %fusion.1), calls=%async_computation.4 | async-start | bytes 262144 | tf_op jit(solution)/shard_map/all_to_all | solution.py:307
